TPU v7x, 256 devices: a whole 4x4x8 slice. The times are simulated.
256 devices in a mesh: seq: 64 (over z, x, core), tp: 4 (over y).
Axes of the slice: x: 4, y: 4, z: 8, core: 2. Of those that a mesh axis runs over, the one named last changes fastest.
Arguments:
- tokens: bfloat16 [32768, 4096], P('seq', 'tp'), may hold values from -6 to 6
- log_decay: float32 [32768, 16], P('seq', 'tp'), may hold values from -2 to 0
- w_query: bfloat16 [4096, 2048], P(None, 'tp'), may hold values from -0.09375 to 0.09375
- w_key: bfloat16 [4096, 512], P(None, 'tp'), may hold values from -0.09375 to 0.09375
- w_value: bfloat16 [4096, 512], P(None, 'tp'), may hold values from -0.09375 to 0.09375
- w_level: bfloat16 [4096, 144], P(None, 'tp'), may hold values from -0.09375 to 0.09375
- w_out: bfloat16 [2048, 4096], P('tp'), may hold values from -0.125 to 0.125
Outputs:
- mixed: bfloat16 [32768, 4096], P('seq', 'tp')
All inputs are finite; a program needn't handle non-finite values.
Results may differ from a plain program's by a relative error of at most 0.02.
Values may be sent and summed in bfloat16 or wider, within the bound.
A program may use at most 128 MiB of HBM per device.

v0:
```python
import jax
import jax.numpy as jnp
from jax import lax
from jax.sharding import PartitionSpec as P

BLOCK = 128
HIGHEST = lax.Precision.HIGHEST
F32 = jnp.float32
BF16 = jnp.bfloat16


def body(tokens, log_decay, w_query, w_key, w_value, w_level, w_out):
    rows = tokens.shape[0]
    heads = log_decay.shape[1]
    size = w_out.shape[0] // heads
    level_count = w_level.shape[1] // heads
    blocks = rows // BLOCK
    local_bits = blocks.bit_length() - 1
    seq_size = lax.axis_size("seq")
    seq_bits = seq_size.bit_length() - 1
    device = lax.axis_index("seq")
    positions = jnp.arange(rows, dtype=jnp.int32)
    triangle = (positions[:, None] >= positions[None, :]).astype(F32)
    decay = jnp.dot(triangle, log_decay, precision=HIGHEST)
    total = decay[rows - 1]

    def swap(x, bit):
        pairs = [(i, i ^ 1 << bit) for i in range(seq_size)]
        return lax.ppermute(x, "seq", pairs)

    group, before = (total, jnp.zeros_like(total))
    befores, fades = ([], [])
    for bit in range(seq_bits):
        upper = jnp.right_shift(device, bit) & 1 == 1
        other = swap(group, bit)
        befores.append(jnp.where(upper, before, -jnp.inf))
        fades.append(jnp.exp(jnp.where(upper, group, other)))
        before = before + jnp.where(upper, other, 0.0)
        group = group + other
    piece = lax.all_gather(tokens, "tp", axis=1, tiled=True)
    dot = lambda a, b: jnp.dot(a, b, preferred_element_type=F32)
    keys = dot(piece, w_key).astype(BF16)
    values = dot(piece, w_value).astype(BF16)
    keep = jnp.exp(total[None, :] - decay)
    weighted = (keep.T[:, :, None] * keys.astype(F32)[None]).astype(BF16)
    state = jnp.einsum("htd,te->hde", weighted, values, preferred_element_type=F32)
    buckets = []
    for bit in range(seq_bits):
        upper = jnp.right_shift(device, bit) & 1 == 1
        other = swap(state.astype(BF16), bit)
        buckets.append(other)
        wide = other.astype(F32)
        low = jnp.where(upper, wide, state)
        high = jnp.where(upper, state, wide)
        state = high + fades[bit][:, None, None] * low
    query = dot(piece, w_query).astype(BF16).reshape(rows, heads, size)
    level = jax.nn.softplus(dot(piece, w_level)).reshape(rows, heads, level_count)
    qb = query.reshape(blocks, BLOCK, heads, size)
    kb = keys.reshape(blocks, BLOCK, size)
    vb = values.reshape(blocks, BLOCK, size)
    lb = level.reshape(blocks, BLOCK, heads, level_count)
    db = decay.reshape(blocks, BLOCK, heads)
    scores = jnp.einsum("cihd,cjd->hcij", qb, kb, preferred_element_type=F32)
    inside = jnp.arange(BLOCK)
    causal = inside[:, None] >= inside[None, :]
    dh = db.transpose(2, 0, 1)
    gaps = jnp.where(causal, dh[:, :, :, None] - dh[:, :, None, :], -jnp.inf)
    mixing = lb[:, :, :, 0].transpose(2, 0, 1)[:, :, :, None] * jnp.exp(gaps) * scores
    out = jnp.einsum("hcij,cje->hcie", mixing.astype(BF16), vb, preferred_element_type=F32)
    ends = db[:, BLOCK - 1]
    weighted = jnp.exp(ends[:, None] - db).transpose(2, 0, 1)[..., None] * kb.astype(F32)[None]
    small = jnp.einsum("hcjd,cje->hcde", weighted.astype(BF16), vb, preferred_element_type=F32)
    small_ends = ends
    parts = [out[:, c] for c in range(blocks)]
    for bit in range(local_bits):
        for c in range(blocks):
            if c >> bit & 1:
                s = (c >> bit) - 1
                factor = lb[c, :, :, 1 + bit] * jnp.exp(db[c] - small_ends[s][None, :])
                got = jnp.einsum(
                    "ihd,hde->hie", qb[c], small[:, s].astype(BF16), preferred_element_type=F32
                )
                parts[c] = parts[c] + factor.T[:, :, None] * got
        fade = jnp.exp(small_ends[1::2] - small_ends[0::2])
        small = small[:, 1::2] + fade.T[:, :, None, None] * small[:, 0::2]
        small_ends = small_ends[1::2]
    combined = jnp.concatenate(parts, axis=1)
    for bit in range(seq_bits):
        factor = level[:, :, 1 + local_bits + bit] * jnp.exp(decay + befores[bit][None, :])
        got = jnp.einsum("thd,hde->hte", query, buckets[bit], preferred_element_type=F32)
        combined = combined + factor.T[:, :, None] * got
    normed = (
        combined * lax.rsqrt(jnp.mean(combined * combined, axis=-1, keepdims=True) + 1e-05)
    ).astype(BF16)
    wide = normed.transpose(1, 0, 2).reshape(rows, heads * size)
    partial = dot(wide, w_out)
    return lax.psum_scatter(partial.astype(BF16), "tp", scatter_dimension=1, tiled=True)


def solution(mesh):
    in_specs = (
        P("seq", "tp"),
        P("seq", "tp"),
        P(None, "tp"),
        P(None, "tp"),
        P(None, "tp"),
        P(None, "tp"),
        P("tp", None),
    )
    return jax.shard_map(
        body, mesh=mesh, in_specs=in_specs, out_specs=P("seq", "tp"), check_vma=False
    )
```

profile of v0, /device:TPU:1, one launch (start us, length us, event | category | flops | bytes accessed | tf_op | source)
XLA Modules:
  0.0 197.4 jit_solution(4253804932975548665)
XLA Ops:
  6.5 0.7 all-gather.2.cloned.1.call-update
  7.3 1.1 fusion.16
  8.7 3.3 %collective-permute-start.1 = (f32[4]{0:T(128)S(1)}, f32[4]{0:T(128)S(1)}, u32[]{:S(2)}, u32[]{:S(2)}) collective-permute-start(f32[4]{0:T(128)S(1)} %slice_reduce_fusion), channel_id=1, source_target_pairs={{0,4},{4,0},{8,12},{12,8},{16,20},{20,16},{24,28},{28,24},{32,36},... | collective-permute-start | bytes 56 | tf_op jit(solution)/shard_map/ppermute | solution.py:29
  12.4 0.7 copy.134
  13.1 0.6 copy.138
  14.4 0.6 iota_compare_fusion.2
  15.6 0.6 fusion.66
  16.2 2.4 %collective-permute-done.3 = f32[4]{0:T(128)S(1)} collective-permute-done((f32[4]{0:T(128)S(1)}, f32[4]{0:T(128)S(1)}, u32[]{:S(2)}, u32[]{:S(2)}) %collective-permute-start.3) | collective-permute-done | bytes 48 | tf_op jit(solution)/shard_map/ppermute | solution.py:29
  19.2 1.0 collective-permute-start.5
  20.2 2.9 %collective-permute-done.5 = f32[4]{0:T(128)S(1)} collective-permute-done((f32[4]{0:T(128)S(1)}, f32[4]{0:T(128)S(1)}, u32[]{:S(2)}, u32[]{:S(2)}) %collective-permute-start.5) | collective-permute-done | bytes 48 | tf_op jit(solution)/shard_map/ppermute | solution.py:29
  23.6 2.4 %collective-permute-done.7 = f32[4]{0:T(128)S(1)} collective-permute-done((f32[4]{0:T(128)S(1)}, f32[4]{0:T(128)S(1)}, u32[]{:S(2)}, u32[]{:S(2)}) %collective-permute-start.7) | collective-permute-done | bytes 48 | tf_op jit(solution)/shard_map/ppermute | solution.py:29
  26.0 0.6 fusion.84
  26.6 1.4 collective-permute-start.9
  28.0 1.9 collective-permute-done.9
  30.5 33.4 %all-gather.2.cloned.1.call-done = bf16[512,4096]{1,0:T(8,128)(2,1)} async-done(((bf16[512,1024]{1,0:T(8,128)(2,1)}), bf16[512,4096]{1,0:T(8,128)(2,1)}) %all-gather.2.cloned.1.call-update) | async-done | bytes 4194320 | tf_op jit(solution)/shard_map/all_gather | solution.py:40
  63.9 3.6 %compare_select_fusion = f32[512,36]{0,1:T(8,128)S(1)} fusion(bf16[512,4096]{1,0:T(8,128)(2,1)} %all-gather.2.cloned.1.call-done, bf16[4096,36]{0,1:T(8,128)(2,1)} %param.12), kind=kOutput, calls=%fused_computation.79 | convolution fusion | flops 151105536 | bytes 4562944 | tf_op jit(solution)/shard_map/dot_general | solution.py:41
  67.6 0.6 fusion.82
  68.2 5.8 %convolution_convert_fusion.1 = bf16[512,512]{0,1:T(8,128)(2,1)S(1)} fusion(bf16[512,4096]{1,0:T(8,128)(2,1)} %all-gather.2.cloned.1.call-done, bf16[4096,512]{1,0:T(8,128)(2,1)} %param.9), kind=kOutput, calls=%fused_computation.17 | convolution fusion | flops 2147745792 | bytes 8912896 | tf_op jit(solution)/shard_map/dot_general | solution.py:41
  74.1 0.8 fusion.80
  74.9 0.7 reshape.80
  76.2 3.4 %convolution_convert_fusion.2 = bf16[512,128]{1,0:T(8,128)(2,1)S(1)} fusion(bf16[512,4096]{1,0:T(8,128)(2,1)} %all-gather.2.cloned.1.call-done, bf16[4096,128]{1,0:T(8,128)(2,1)S(1)} %copy-done), kind=kOutput, calls=%fused_computation.27 | convolution fusion | flops 536936448 | bytes 5373952 | tf_op jit(solution)/shard_map/dot_general | solution.py:41
  79.8 3.7 %convolution_convert_fusion.3 = bf16[512,128]{1,0:T(8,128)(2,1)S(1)} fusion(bf16[512,4096]{1,0:T(8,128)(2,1)} %all-gather.2.cloned.1.call-done, bf16[4096,128]{1,0:T(8,128)(2,1)} %param.11), kind=kOutput, calls=%fused_computation.28 | convolution fusion | flops 536936448 | bytes 5373952 | tf_op jit(solution)/shard_map/dot_general | solution.py:41
  83.6 0.9 fusion.87
  84.6 1.2 fusion.81
  85.9 0.7 fusion.57
  86.6 1.0 fusion.86
  87.5 0.7 collective-permute-start
  88.4 2.8 %convolution_bitcast_fusion.1 = f32[4,4,128,128]{3,2,0,1:T(8,128)} fusion(bf16[4,128,128,1]{2,1,3,0:T(8,128)(2,1)} %bitcast.198, bf16[4,128,128,1]{2,1,3,0:T(8,128)(2,1)S(1)} %bitcast.194, bf16[4,128,4,128]{1,0,3,2:T(4,128)(2,1)S(1)} %reshape_reshape.7, f32[4,4,128]{2,0,1:T(4,128)} %copy.55, f32[4,4,128]{2,0,1:T(4,128)} %copy.54, ...), kind=kOutput, calls=%fused_computation.14 | convolution fusion | flops 135528448 | bytes 1867776 | tf_op jit(solution)/shard_map/hcij,cje->hcie/dot_general | solution.py:69
  91.2 0.8 fusion.63
  92.0 1.2 fusion.9
  93.4 1.3 fusion.10
  94.7 1.3 fusion.11
  96.0 0.8 fusion.74
  96.8 1.3 collective-permute-start.2
  98.1 1.0 slice_bitcast_fusion.3
  99.0 3.0 %collective-permute-done.2 = bf16[4,128,128]{2,1,0:T(8,128)(2,1)S(1)} collective-permute-done((bf16[4,128,128]{2,1,0:T(8,128)(2,1)S(1)}, bf16[4,128,128]{2,1,0:T(8,128)(2,1)S(1)}, u32[]{:S(2)}, u32[]{:S(2)}) %collective-permute-start.2) | collective-permute-done | bytes 131104 | tf_op jit(solution)/shard_map/ppermute | solution.py:29
  102.0 0.8 fusion.43
  102.8 2.8 %collective-permute-start.4 = (bf16[4,128,128]{2,1,0:T(8,128)(2,1)S(1)}, bf16[4,128,128]{2,1,0:T(8,128)(2,1)S(1)}, u32[]{:S(2)}, u32[]{:S(2)}) collective-permute-start(bf16[4,128,128]{2,1,0:T(8,128)(2,1)S(1)} %fusion.43), channel_id=1, source_target_pairs={{0,16},{4,20},{8,24},{12,28},{16,0},{20,4},{24,8},{28,12},{32,48},... | collective-permute-start | bytes 393224 | tf_op jit(solution)/shard_map/ppermute | solution.py:29
  106.1 2.5 %collective-permute-done.4 = bf16[4,128,128]{2,1,0:T(8,128)(2,1)S(1)} collective-permute-done((bf16[4,128,128]{2,1,0:T(8,128)(2,1)S(1)}, bf16[4,128,128]{2,1,0:T(8,128)(2,1)S(1)}, u32[]{:S(2)}, u32[]{:S(2)}) %collective-permute-start.4) | collective-permute-done | bytes 131104 | tf_op jit(solution)/shard_map/ppermute | solution.py:29
  108.9 1.4 collective-permute-start.6
  110.8 2.0 %collective-permute-done.6 = bf16[4,128,128]{2,1,0:T(8,128)(2,1)S(1)} collective-permute-done((bf16[4,128,128]{2,1,0:T(8,128)(2,1)S(1)}, bf16[4,128,128]{2,1,0:T(8,128)(2,1)S(1)}, u32[]{:S(2)}, u32[]{:S(2)}) %collective-permute-start.6) | collective-permute-done | bytes 131104 | tf_op jit(solution)/shard_map/ppermute | solution.py:29
  112.9 2.3 %collective-permute-start.8 = (bf16[4,128,128]{2,1,0:T(8,128)(2,1)S(1)}, bf16[4,128,128]{2,1,0:T(8,128)(2,1)S(1)}, u32[]{:S(2)}, u32[]{:S(2)}) collective-permute-start(bf16[4,128,128]{2,1,0:T(8,128)(2,1)S(1)} %fusion.42), channel_id=1, source_target_pairs={{0,64},{4,68},{8,72},{12,76},{16,80},{20,84},{24,88},{28,92},{32,9... | collective-permute-start | bytes 393224 | tf_op jit(solution)/shard_map/ppermute | solution.py:29
  115.8 3.4 %collective-permute-done.8 = bf16[4,128,128]{2,1,0:T(8,128)(2,1)S(1)} collective-permute-done((bf16[4,128,128]{2,1,0:T(8,128)(2,1)S(1)}, bf16[4,128,128]{2,1,0:T(8,128)(2,1)S(1)}, u32[]{:S(2)}, u32[]{:S(2)}) %collective-permute-start.8) | collective-permute-done | bytes 131104 | tf_op jit(solution)/shard_map/ppermute | solution.py:29
  119.3 5.5 %collective-permute-start.10 = (bf16[4,128,128]{2,1,0:T(8,128)(2,1)S(1)}, bf16[4,128,128]{2,1,0:T(8,128)(2,1)S(1)}, u32[]{:S(2)}, u32[]{:S(2)}) collective-permute-start(bf16[4,128,128]{2,1,0:T(8,128)(2,1)S(1)} %fusion.39), channel_id=1, source_target_pairs={{0,128},{4,132},{8,136},{12,140},{16,144},{20,148},{24,152},{28,15... | collective-permute-start | bytes 393224 | tf_op jit(solution)/shard_map/ppermute | solution.py:29
  125.3 2.0 collective-permute-done.10
  127.8 1.1 multiply_reduce_fusion
  129.5 6.5 %convolution_convert_fusion = bf16[512,4096]{1,0:T(8,128)(2,1)} fusion(bf16[512,512]{0,1:T(8,128)(2,1)S(1)} %bitcast.190, bf16[512,4096]{1,0:T(8,128)(2,1)} %param.13), kind=kOutput, calls=%fused_computation | convolution fusion | flops 2149580800 | bytes 8912896 | tf_op jit(solution)/shard_map/dot_general | solution.py:41
  136.0 54.5 %reduce-scatter.2.cloned.1.call-done = bf16[512,1024]{1,0:T(8,128)(2,1)} async-done(((bf16[512,4096]{1,0:T(8,128)(2,1)}), bf16[512,1024]{1,0:T(8,128)(2,1)}) %reduce-scatter.2.cloned.1.call-update) | async-done | bytes 1048592 | tf_op jit(solution)/shard_map/reduce_scatter | solution.py:97
  (85 shorter events, 8.6 us)
Async XLA Ops:
  6.5 69.7 %copy-start = (bf16[4096,128]{1,0:T(8,128)(2,1)S(1)}, bf16[4096,128]{1,0:T(8,128)(2,1)}, u32[]{:S(2)}) copy-start(bf16[4096,128]{1,0:T(8,128)(2,1)} %param.10) | copy-start | bytes 3145732
  6.5 57.3 %all-gather.2.cloned.1.call-start = ((), (), s32[]{:S(2)}) async-start(), calls=%async_computation.1 | async-start | bytes 5242880 | tf_op jit(solution)/shard_map/all_gather | solution.py:40
  7.3 183.3 %reduce-scatter.2.cloned.1.call-start = ((), (), s32[]{:S(2)}) async-start(), calls=%async_computation.2 | async-start | bytes 5242880 | tf_op jit(solution)/shard_map/reduce_scatter | solution.py:97
  8.6 55.2 %copy-start.9 = (f32[4]{0:T(128)}, f32[4]{0:T(128)S(1)}, u32[]{:S(2)}) copy-start(f32[4]{0:T(128)S(1)} %slice_reduce_fusion) | copy-start | bytes 52
  8.7 6.9 %collective-permute-start.1 = (f32[4]{0:T(128)S(1)}, f32[4]{0:T(128)S(1)}, u32[]{:S(2)}, u32[]{:S(2)}) collective-permute-start(f32[4]{0:T(128)S(1)} %slice_reduce_fusion), channel_id=1, source_target_pairs={{0,4},{4,0},{8,12},{12,8},{16,20},{20,16},{24,28},{28,24},{32,36},... | collective-permute-start | bytes 56 | tf_op jit(solution)/shard_map/ppermute | solution.py:29
  14.4 1.8 copy-start.19
  16.2 2.4 %collective-permute-start.3 = (f32[4]{0:T(128)S(1)}, f32[4]{0:T(128)S(1)}, u32[]{:S(2)}, u32[]{:S(2)}) collective-permute-start(f32[4]{0:T(128)S(1)} %get-tuple-element.50), channel_id=1, source_target_pairs={{0,8},{4,12},{8,0},{12,4},{16,24},{20,28},{24,16},{28,20},{32,40},... | collective-permute-start | bytes 56 | tf_op jit(solution)/shard_map/ppermute | solution.py:29
  19.2 3.9 %collective-permute-start.5 = (f32[4]{0:T(128)S(1)}, f32[4]{0:T(128)S(1)}, u32[]{:S(2)}, u32[]{:S(2)}) collective-permute-start(f32[4]{0:T(128)S(1)} %get-tuple-element.55), channel_id=1, source_target_pairs={{0,16},{4,20},{8,24},{12,28},{16,0},{20,4},{24,8},{28,12},{32,48},... | collective-permute-start | bytes 56 | tf_op jit(solution)/shard_map/ppermute | solution.py:29
  23.6 2.4 %collective-permute-start.7 = (f32[4]{0:T(128)S(1)}, f32[4]{0:T(128)S(1)}, u32[]{:S(2)}, u32[]{:S(2)}) collective-permute-start(f32[4]{0:T(128)S(1)} %get-tuple-element.45), channel_id=1, source_target_pairs={{0,32},{4,36},{8,40},{12,44},{16,48},{20,52},{24,56},{28,60},{32,0... | collective-permute-start | bytes 56 | tf_op jit(solution)/shard_map/ppermute | solution.py:29
  26.6 3.3 %collective-permute-start.9 = (f32[4]{0:T(128)S(1)}, f32[4]{0:T(128)S(1)}, u32[]{:S(2)}, u32[]{:S(2)}) collective-permute-start(f32[4]{0:T(128)S(1)} %get-tuple-element.43), channel_id=1, source_target_pairs={{0,64},{4,68},{8,72},{12,76},{16,80},{20,84},{24,88},{28,92},{32,9... | collective-permute-start | bytes 56 | tf_op jit(solution)/shard_map/ppermute | solution.py:29
  79.8 6.0 %copy-start.10 = (f32[4]{0:T(128)S(1)}, f32[4]{0:T(128)}, u32[]{:S(2)}) copy-start(f32[4]{0:T(128)} %copy-done.9) | copy-start | bytes 52
  79.8 6.0 %copy-start.14 = (f32[4]{0:T(128)S(1)}, f32[4]{0:T(128)}, u32[]{:S(2)}) copy-start(f32[4]{0:T(128)} %get-tuple-element.54) | copy-start | bytes 52
  79.8 6.0 %copy-start.15 = (f32[4]{0:T(128)S(1)}, f32[4]{0:T(128)}, u32[]{:S(2)}) copy-start(f32[4]{0:T(128)} %get-tuple-element.5) | copy-start | bytes 52
  79.8 6.0 %copy-start.16 = (f32[4]{0:T(128)S(1)}, f32[4]{0:T(128)}, u32[]{:S(2)}) copy-start(f32[4]{0:T(128)} %get-tuple-element.51) | copy-start | bytes 52
  79.8 6.0 %copy-start.17 = (f32[4]{0:T(128)S(1)}, f32[4]{0:T(128)}, u32[]{:S(2)}) copy-start(f32[4]{0:T(128)} %get-tuple-element.41) | copy-start | bytes 52
  79.8 6.0 %copy-start.18 = (f32[4]{0:T(128)S(1)}, f32[4]{0:T(128)}, u32[]{:S(2)}) copy-start(f32[4]{0:T(128)} %get-tuple-element.42) | copy-start | bytes 52
  79.8 8.4 %slice-start = ((f32[4,2]{0,1:T(2,128)}), f32[4,1]{0,1:T(1,128)S(1)}, s32[]{:S(2)}) async-start(f32[4,2]{0,1:T(2,128)} %copy-done.19), calls=%async_computation.3 | async-start | bytes 1024 | tf_op jit(solution)/shard_map/slice | solution.py:81
  83.6 3.9 %copy-start.1 = (bf16[512,128]{1,0:T(8,128)(2,1)}, bf16[512,128]{1,0:T(8,128)(2,1)S(1)}, u32[]{:S(2)}) copy-start(bf16[512,128]{1,0:T(8,128)(2,1)S(1)} %convolution_convert_fusion.3) | copy-start | bytes 393220
  87.5 18.1 %copy-start.5 = (f32[4,512]{1,0:T(4,128)S(1)}, f32[4,512]{1,0:T(4,128)}, u32[]{:S(2)}) copy-start(f32[4,512]{1,0:T(4,128)} %get-tuple-element.33) | copy-start | bytes 24580
  87.5 8.5 %collective-permute-start = (bf16[4,128,128]{2,1,0:T(8,128)(2,1)}, bf16[4,128,128]{2,1,0:T(8,128)(2,1)S(1)}, u32[]{:S(2)}, u32[]{:S(2)}) collective-permute-start(bf16[4,128,128]{2,1,0:T(8,128)(2,1)} %get-tuple-element.57), channel_id=1, source_target_pairs={{0,4},{4,0},{8,12},{12,8},{16,20},{20,16},{24,28},{28,24},{32,36},... | collective-permute-start | bytes 393224 | tf_op jit(solution)/shard_map/ppermute | solution.py:29
  88.3 20.3 %copy-start.7 = (f32[4]{0:T(128)S(1)}, f32[4]{0:T(128)}, u32[]{:S(2)}) copy-start(f32[4]{0:T(128)} %get-tuple-element.49) | copy-start | bytes 52
  88.4 20.3 %copy-start.8 = (f32[4]{0:T(128)S(1)}, f32[4]{0:T(128)}, u32[]{:S(2)}) copy-start(f32[4]{0:T(128)} %get-tuple-element.56) | copy-start | bytes 52
  88.4 20.3 %copy-start.12 = (f32[4]{0:T(128)S(1)}, f32[4]{0:T(128)}, u32[]{:S(2)}) copy-start(f32[4]{0:T(128)} %get-tuple-element.46) | copy-start | bytes 52
  91.2 19.1 %copy-start.4 = (f32[4,512]{1,0:T(4,128)S(1)}, f32[4,512]{1,0:T(4,128)}, u32[]{:S(2)}) copy-start(f32[4,512]{1,0:T(4,128)} %get-tuple-element.32) | copy-start | bytes 24580
  93.2 19.6 %copy-start.11 = (f32[4]{0:T(128)S(1)}, f32[4]{0:T(128)}, u32[]{:S(2)}) copy-start(f32[4]{0:T(128)} %get-tuple-element.44) | copy-start | bytes 52
  93.4 21.8 %copy-start.3 = (f32[4,512]{1,0:T(4,128)S(1)}, f32[4,512]{1,0:T(4,128)}, u32[]{:S(2)}) copy-start(f32[4,512]{1,0:T(4,128)} %get-tuple-element.31) | copy-start | bytes 24580
  96.0 23.1 %copy-start.13 = (f32[4]{0:T(128)S(1)}, f32[4]{0:T(128)}, u32[]{:S(2)}) copy-start(f32[4]{0:T(128)} %get-tuple-element.53) | copy-start | bytes 52
  96.8 28.0 %copy-start.2 = (f32[4,512]{1,0:T(4,128)S(1)}, f32[4,512]{1,0:T(4,128)}, u32[]{:S(2)}) copy-start(f32[4,512]{1,0:T(4,128)} %get-tuple-element.30) | copy-start | bytes 24580
  96.8 5.2 %collective-permute-start.2 = (bf16[4,128,128]{2,1,0:T(8,128)(2,1)S(1)}, bf16[4,128,128]{2,1,0:T(8,128)(2,1)S(1)}, u32[]{:S(2)}, u32[]{:S(2)}) collective-permute-start(bf16[4,128,128]{2,1,0:T(8,128)(2,1)S(1)} %fusion.74), channel_id=1, source_target_pairs={{0,8},{4,12},{8,0},{12,4},{16,24},{20,28},{24,16},{28,20},{32,40},... | collective-permute-start | bytes 393224 | tf_op jit(solution)/shard_map/ppermute | solution.py:29
  102.8 5.8 %collective-permute-start.4 = (bf16[4,128,128]{2,1,0:T(8,128)(2,1)S(1)}, bf16[4,128,128]{2,1,0:T(8,128)(2,1)S(1)}, u32[]{:S(2)}, u32[]{:S(2)}) collective-permute-start(bf16[4,128,128]{2,1,0:T(8,128)(2,1)S(1)} %fusion.43), channel_id=1, source_target_pairs={{0,16},{4,20},{8,24},{12,28},{16,0},{20,4},{24,8},{28,12},{32,48},... | collective-permute-start | bytes 393224 | tf_op jit(solution)/shard_map/ppermute | solution.py:29
  108.9 18.9 %copy-start.6 = (f32[4,512]{1,0:T(4,128)S(1)}, f32[4,512]{1,0:T(4,128)}, u32[]{:S(2)}) copy-start(f32[4,512]{1,0:T(4,128)} %get-tuple-element.28) | copy-start | bytes 24580
  108.9 3.9 %collective-permute-start.6 = (bf16[4,128,128]{2,1,0:T(8,128)(2,1)S(1)}, bf16[4,128,128]{2,1,0:T(8,128)(2,1)S(1)}, u32[]{:S(2)}, u32[]{:S(2)}) collective-permute-start(bf16[4,128,128]{2,1,0:T(8,128)(2,1)S(1)} %get-tuple-element.9), channel_id=1, source_target_pairs={{0,32},{4,36},{8,40},{12,44},{16,48},{20,52},{24,56},{28,60},{32,0... | collective-permute-start | bytes 393224 | tf_op jit(solution)/shard_map/ppermute | solution.py:29
  112.9 6.2 %collective-permute-start.8 = (bf16[4,128,128]{2,1,0:T(8,128)(2,1)S(1)}, bf16[4,128,128]{2,1,0:T(8,128)(2,1)S(1)}, u32[]{:S(2)}, u32[]{:S(2)}) collective-permute-start(bf16[4,128,128]{2,1,0:T(8,128)(2,1)S(1)} %fusion.42), channel_id=1, source_target_pairs={{0,64},{4,68},{8,72},{12,76},{16,80},{20,84},{24,88},{28,92},{32,9... | collective-permute-start | bytes 393224 | tf_op jit(solution)/shard_map/ppermute | solution.py:29
  119.3 8.0 %collective-permute-start.10 = (bf16[4,128,128]{2,1,0:T(8,128)(2,1)S(1)}, bf16[4,128,128]{2,1,0:T(8,128)(2,1)S(1)}, u32[]{:S(2)}, u32[]{:S(2)}) collective-permute-start(bf16[4,128,128]{2,1,0:T(8,128)(2,1)S(1)} %fusion.39), channel_id=1, source_target_pairs={{0,128},{4,132},{8,136},{12,140},{16,144},{20,148},{24,152},{28,15... | collective-permute-start | bytes 393224 | tf_op jit(solution)/shard_map/ppermute | solution.py:29
Sparse Core Ops, SparseCore 0:
  9.2 54.6 all-gather.1
  136.1 54.3 reduce-scatter.1
where the time goes:
time: 198 us; the launch traced here: 197 us
  waiting for transfers between devices  111 us (56%)
  matrix products  36.4 us (18%)
  starting transfers between devices  19.8 us (10%)
  between operations  13.9 us (7%)
  local copies, waits for them, and re-layouts  8.63 us (4%)
  other arithmetic  7.64 us (4%)
    reduce_scatter x1, waiting for transfers between devices, body(): lax.psum_scatter(partial.astype(BF16), 'tp', scatter_dimension=1, tiled=T...  54.5 us
    all_gather x1, waiting for transfers between devices, body(): piece = lax.all_gather(tokens, 'tp', axis=1, tiled=True)  33.4 us
    dot_general x5, matrix products, body(): dot = lambda a, b: jnp.dot(a, b, preferred_element_type=F32)  23.2 us
    ppermute x11, waiting for transfers between devices, swap(): return lax.ppermute(x, 'seq', pairs)  22.4 us
    ppermute x11, starting transfers between devices, swap(): return lax.ppermute(x, 'seq', pairs)  19.8 us
    dot_general x4, matrix products, body(): jnp.einsum('ihd,hde->hie', qb[c], small[:, s].astype(BF16), preferred_ele...  3.96 us
  transfers between devices with their start and end apart: 13, of which 11 were waited for; matrix products, arithmetic and copies ran while one was open for 9% of the time, Pallas kernels for 0%

commit v1 on v0

--- a/solution.py
+++ b/solution.py
@@ -1,12 +1,46 @@
+import functools
 import jax
 import jax.numpy as jnp
 from jax import lax
 from jax.sharding import PartitionSpec as P
+from jax.lax import axis_index, axis_size, ppermute
 
 BLOCK = 128
 HIGHEST = lax.Precision.HIGHEST
 F32 = jnp.float32
 BF16 = jnp.bfloat16
+
+
+def resolve_limits(slab_in, axis_no):
+    slab_in = jnp.moveaxis(slab_in, 0, axis_no)
+    carry_out = slab_in.shape
+    t1 = slab_in.reshape(
+        *carry_out[:axis_no], carry_out[axis_no] * carry_out[axis_no + 1], *carry_out[axis_no + 2 :]
+    )
+    return t1
+
+
+def case_open(inputs, mesh_ax, k_dim):
+    sides = axis_size(mesh_ax)
+    series = tuple(((q, (q + 1) % sides) for q in range(sides)))
+    lanes = tuple(((nth, pp) for pp, nth in series))
+    last, answer = ([], [])
+    for p in range(sides - 1):
+        if p % 2 == 0:
+            found_now = ppermute(last[-1] if last else inputs, axis_name=mesh_ax, perm=series)
+            last.append(found_now)
+        else:
+            answer.append(ppermute(answer[-1] if answer else inputs, mesh_ax, perm=lanes))
+    block_next = jnp.stack([*last[::-1], inputs, *answer], 0)
+    ready = axis_index(mesh_ax)
+    taken_in = len(last)
+    state_next = ready - taken_in
+    block_next = block_next[(jnp.arange(sides) - state_next) % sides]
+    newest = resolve_limits(block_next, k_dim)
+    return newest
+
+
+part_the_edges = functools.partial(case_open, mesh_ax="tp", k_dim=1)
 
 
 def body(tokens, log_decay, w_query, w_key, w_value, w_level, w_out):
@@ -37,7 +71,7 @@
         fades.append(jnp.exp(jnp.where(upper, group, other)))
         before = before + jnp.where(upper, other, 0.0)
         group = group + other
-    piece = lax.all_gather(tokens, "tp", axis=1, tiled=True)
+    piece = part_the_edges(tokens)
     dot = lambda a, b: jnp.dot(a, b, preferred_element_type=F32)
     keys = dot(piece, w_key).astype(BF16)
     values = dot(piece, w_value).astype(BF16)

time: 198 us -> 207 us (1.045)
  waiting for transfers between devices: 111 us -> 88.2 us
  starting transfers between devices: 19.8 us -> 37.6 us
  local copies, waits for them, and re-layouts: 8.63 us -> 20.3 us
  other arithmetic: 7.64 us -> 11.4 us
    all_gather x1 -> x0, waiting for transfers between devices: 33.4 us -> none  [body(): piece = lax.all_gather(tokens, 'tp', axis=1, tiled=True)]
    ppermute x0 -> x3, waiting for transfers between devices: none -> 18.3 us  [the longest x2 18.3 us: case_open(): ppermute(last[-1] if last else inputs, axis_name=mesh_ax, perm=series)]
    ppermute x11, starting transfers between devices: 19.8 us -> 32.4 us  [swap(): return lax.ppermute(x, 'seq', pairs)]
    transpose x0 -> x1, local copies, waits for them, and re-layouts: none -> 6.23 us  [resolve_limits(): slab_in = jnp.moveaxis(slab_in, 0, axis_no)]
    ppermute x11, waiting for transfers between devices: 22.4 us -> 16.9 us  [swap(): return lax.ppermute(x, 'seq', pairs)]
    ppermute x0 -> x3, starting transfers between devices: none -> 5.13 us  [the longest x2 3.69 us: case_open(): ppermute(last[-1] if last else inputs, axis_name=mesh_ax, perm=series)]
    gather x0 -> x1, local copies, waits for them, and re-layouts: none -> 5.04 us  [case_open(): block_next = block_next[(jnp.arange(sides) - state_next) % sides]]
    another operation x0 -> x1, other arithmetic: none -> 3.32 us  [case_open(): block_next = jnp.stack([*last[::-1], inputs, *answer], 0)]
  transfers between devices with their start and end apart: 13 -> 15, of which waited for: 11 -> 12; matrix products, arithmetic and copies ran while one was open for 9% -> 9% of each run, Pallas kernels for 0% -> 0%
where the time goes in v1:
time: 207 us; the launch traced here: 206 us
  waiting for transfers between devices  88.2 us (43%)
  starting transfers between devices  37.6 us (18%)
  matrix products  34.7 us (17%)
  local copies, waits for them, and re-layouts  20.3 us (10%)
  between operations  13.8 us (7%)
  other arithmetic  11.4 us (6%)
    reduce_scatter x1, waiting for transfers between devices, body(): lax.psum_scatter(partial.astype(BF16), 'tp', scatter_dimension=1, tiled=T...  53 us
    ppermute x11, starting transfers between devices, swap(): return lax.ppermute(x, 'seq', pairs)  32.4 us
    dot_general x5, matrix products, body(): dot = lambda a, b: jnp.dot(a, b, preferred_element_type=F32)  21.7 us
    ppermute x2, waiting for transfers between devices, case_open(): ppermute(last[-1] if last else inputs, axis_name=mesh_ax, perm=series)  18.3 us
    ppermute x11, waiting for transfers between devices, swap(): return lax.ppermute(x, 'seq', pairs)  16.9 us
    transpose x1, local copies, waits for them, and re-layouts, resolve_limits(): slab_in = jnp.moveaxis(slab_in, 0, axis_no)  6.23 us
    gather x1, local copies, waits for them, and re-layouts, case_open(): block_next = block_next[(jnp.arange(sides) - state_next) % sides]  5.04 us
  transfers between devices with their start and end apart: 15, of which 12 were waited for; matrix products, arithmetic and copies ran while one was open for 9% of the time, Pallas kernels for 0%

profile of v1, /device:TPU:1, one launch (start us, length us, event | category | flops | bytes accessed | tf_op | source)
XLA Modules:
  0.0 205.9 jit_solution(3673473143288593350)
XLA Ops:
  6.5 2.1 %collective-permute-start = (bf16[512,1024]{1,0:T(8,128)(2,1)}, bf16[512,1024]{1,0:T(8,128)(2,1)S(1)}, u32[]{:S(2)}, u32[]{:S(2)}) collective-permute-start(bf16[512,1024]{1,0:T(8,128)(2,1)} %param.7), channel_id=1, source_target_pairs={{0,1},{1,2},{2,3},{3,0},{4,5},{5,6},{6,7},{7,4},{8,9},{9,10},{10,1... | collective-permute-start | bytes 3145736 | tf_op jit(solution)/shard_map/ppermute | solution.py:30
  8.7 1.4 collective-permute-start.2
  10.1 1.1 fusion.16
  11.5 3.0 %collective-permute-start.4 = (f32[4]{0:T(128)S(1)}, f32[4]{0:T(128)S(1)}, u32[]{:S(2)}, u32[]{:S(2)}) collective-permute-start(f32[4]{0:T(128)S(1)} %slice_reduce_fusion), channel_id=1, source_target_pairs={{0,4},{4,0},{8,12},{12,8},{16,20},{20,16},{24,28},{28,24},{32,36},... | collective-permute-start | bytes 56 | tf_op jit(solution)/shard_map/ppermute | solution.py:63
  18.5 12.6 %collective-permute-done = bf16[512,1024]{1,0:T(8,128)(2,1)S(1)} collective-permute-done((bf16[512,1024]{1,0:T(8,128)(2,1)}, bf16[512,1024]{1,0:T(8,128)(2,1)S(1)}, u32[]{:S(2)}, u32[]{:S(2)}) %collective-permute-start) | collective-permute-done | bytes 1048608 | tf_op jit(solution)/shard_map/ppermute | solution.py:30
  31.2 1.6 collective-permute-start.1
  33.3 1.4 collective-permute-start.6
  34.7 0.9 collective-permute-done.6
  36.2 3.0 %collective-permute-start.8 = (f32[4]{0:T(128)S(1)}, f32[4]{0:T(128)S(1)}, u32[]{:S(2)}, u32[]{:S(2)}) collective-permute-start(f32[4]{0:T(128)S(1)} %get-tuple-element.55), channel_id=1, source_target_pairs={{0,16},{4,20},{8,24},{12,28},{16,0},{20,4},{24,8},{28,12},{32,48},... | collective-permute-start | bytes 56 | tf_op jit(solution)/shard_map/ppermute | solution.py:63
  39.2 0.9 collective-permute-done.8
  40.7 1.9 collective-permute-start.10
  42.6 1.2 collective-permute-done.10
  44.3 3.0 %collective-permute-start.12 = (f32[4]{0:T(128)S(1)}, f32[4]{0:T(128)S(1)}, u32[]{:S(2)}, u32[]{:S(2)}) collective-permute-start(f32[4]{0:T(128)S(1)} %get-tuple-element.43), channel_id=1, source_target_pairs={{0,64},{4,68},{8,72},{12,76},{16,80},{20,84},{24,88},{28,92},{32,9... | collective-permute-start | bytes 56 | tf_op jit(solution)/shard_map/ppermute | solution.py:63
  47.3 1.2 collective-permute-done.12
  49.1 5.6 %collective-permute-done.1 = bf16[512,1024]{1,0:T(8,128)(2,1)S(1)} collective-permute-done((bf16[512,1024]{1,0:T(8,128)(2,1)S(1)}, bf16[512,1024]{1,0:T(8,128)(2,1)S(1)}, u32[]{:S(2)}, u32[]{:S(2)}) %collective-permute-start.1) | collective-permute-done | bytes 1048608 | tf_op jit(solution)/shard_map/ppermute | solution.py:30
  54.8 3.3 %pad_maximum_fusion = bf16[4,512,1024]{2,1,0:T(8,128)(2,1)} fusion(bf16[1,512,1024]{2,1,0:T(8,128)(2,1)S(1)} %bitcast.208, bf16[1,512,1024]{2,1,0:T(8,128)(2,1)} %bitcast.206, bf16[1,512,1024]{2,1,0:T(8,128)(2,1)S(1)} %bitcast.207, bf16[1,512,1024]{2,1,0:T(8,128)(2,1)S(1)} %bitcast.209), kind=kLoop, calls=%fused_computation.2 | loop fusion | flops 6291456 | bytes 8388608 | tf_op jit(solution)/shard_map/stack | solution.py:34
  58.1 5.0 %gather_fusion = bf16[4,512,1024]{2,1,0:T(8,128)(2,1)} fusion(bf16[4,512,1024]{2,1,0:T(8,128)(2,1)} %pad_maximum_fusion, s32[1024]{0:T(1024)S(1)} %pad_clamp_fusion), kind=kCustom, calls=%fused_computation | custom fusion | bytes 8388624 | tf_op jit(solution)/shard_map/gather | solution.py:38
  63.1 6.2 %copy.101 = bf16[512,4,1024]{0,2,1:T(8,128)(2,1)} copy(bf16[512,4,1024]{2,0,1:T(8,128)(2,1)} %bitcast.202) | data formatting | bytes 8388608 | tf_op jit(solution)/shard_map/transpose | solution.py:15
  69.4 3.0 %compare_select_fusion = f32[512,36]{0,1:T(8,128)S(1)} fusion(bf16[512,4096]{0,1:T(8,128)(2,1)} %bitcast.198, bf16[4096,36]{0,1:T(8,128)(2,1)S(1)} %copy-done.3), kind=kOutput, calls=%fused_computation.81 | convolution fusion | flops 151105536 | bytes 4562944 | tf_op jit(solution)/shard_map/dot_general | solution.py:75
  73.0 5.8 %convolution_convert_fusion.1 = bf16[512,512]{0,1:T(8,128)(2,1)S(1)} fusion(bf16[512,4096]{0,1:T(8,128)(2,1)} %bitcast.199, bf16[4096,512]{1,0:T(8,128)(2,1)} %param.9), kind=kOutput, calls=%fused_computation.19 | convolution fusion | flops 2147745792 | bytes 8912896 | tf_op jit(solution)/shard_map/dot_general | solution.py:75
  79.0 0.8 fusion.82
  81.0 3.8 %convolution_convert_fusion.2 = bf16[512,128]{1,0:T(8,128)(2,1)S(1)} fusion(bf16[512,4096]{0,1:T(8,128)(2,1)} %bitcast.200, bf16[4096,128]{1,0:T(8,128)(2,1)S(1)} %copy-done), kind=kOutput, calls=%fused_computation.29 | convolution fusion | flops 536936448 | bytes 5373952 | tf_op jit(solution)/shard_map/dot_general | solution.py:75
  84.8 2.5 %convolution_convert_fusion.3 = bf16[512,128]{1,0:T(8,128)(2,1)S(1)} fusion(bf16[512,4096]{0,1:T(8,128)(2,1)S(1)} %bitcast.201, bf16[4096,128]{1,0:T(8,128)(2,1)} %param.11), kind=kOutput, calls=%fused_computation.30 | convolution fusion | flops 536936448 | bytes 5373952 | tf_op jit(solution)/shard_map/dot_general | solution.py:75
  87.6 0.9 fusion.89
  88.5 1.2 fusion.83
  89.8 1.4 fusion.57
  91.2 1.0 fusion.88
  92.1 3.7 %collective-permute-start.3 = (bf16[4,128,128]{2,1,0:T(8,128)(2,1)}, bf16[4,128,128]{2,1,0:T(8,128)(2,1)S(1)}, u32[]{:S(2)}, u32[]{:S(2)}) collective-permute-start(bf16[4,128,128]{2,1,0:T(8,128)(2,1)} %get-tuple-element.57), channel_id=1, source_target_pairs={{0,4},{4,0},{8,12},{12,8},{16,20},{20,16},{24,28},{28,24},{32,36},... | collective-permute-start | bytes 393224 | tf_op jit(solution)/shard_map/ppermute | solution.py:63
  95.9 2.6 %convolution_bitcast_fusion.1 = f32[4,4,128,128]{3,2,0,1:T(8,128)} fusion(bf16[4,128,128,1]{2,1,3,0:T(8,128)(2,1)} %bitcast.215, bf16[4,128,128,1]{2,1,3,0:T(8,128)(2,1)S(1)} %bitcast.211, bf16[4,128,4,128]{1,0,3,2:T(4,128)(2,1)S(1)} %reshape_reshape.7, f32[4,4,128]{2,0,1:T(4,128)} %copy.103, f32[4,4,128]{2,0,1:T(4,128)} %copy.102, ...), kind=kOutput, calls=%fused_computation.16 | convolution fusion | flops 135528448 | bytes 1867776 | tf_op jit(solution)/shard_map/hcij,cje->hcie/dot_general | solution.py:103
  98.5 0.8 fusion.63
  99.3 1.2 fusion.9
  100.8 1.3 fusion.10
  102.0 1.3 fusion.11
  104.0 2.6 %collective-permute-start.5 = (bf16[4,128,128]{2,1,0:T(8,128)(2,1)S(1)}, bf16[4,128,128]{2,1,0:T(8,128)(2,1)S(1)}, u32[]{:S(2)}, u32[]{:S(2)}) collective-permute-start(bf16[4,128,128]{2,1,0:T(8,128)(2,1)S(1)} %fusion.76), channel_id=1, source_target_pairs={{0,8},{4,12},{8,0},{12,4},{16,24},{20,28},{24,16},{28,20},{32,40},... | collective-permute-start | bytes 393224 | tf_op jit(solution)/shard_map/ppermute | solution.py:63
  106.6 1.0 slice_bitcast_fusion.3
  107.6 2.9 %collective-permute-done.5 = bf16[4,128,128]{2,1,0:T(8,128)(2,1)S(1)} collective-permute-done((bf16[4,128,128]{2,1,0:T(8,128)(2,1)S(1)}, bf16[4,128,128]{2,1,0:T(8,128)(2,1)S(1)}, u32[]{:S(2)}, u32[]{:S(2)}) %collective-permute-start.5) | collective-permute-done | bytes 131104 | tf_op jit(solution)/shard_map/ppermute | solution.py:63
  110.5 0.8 fusion.43
  111.2 2.9 %collective-permute-start.7 = (bf16[4,128,128]{2,1,0:T(8,128)(2,1)S(1)}, bf16[4,128,128]{2,1,0:T(8,128)(2,1)S(1)}, u32[]{:S(2)}, u32[]{:S(2)}) collective-permute-start(bf16[4,128,128]{2,1,0:T(8,128)(2,1)S(1)} %fusion.43), channel_id=1, source_target_pairs={{0,16},{4,20},{8,24},{12,28},{16,0},{20,4},{24,8},{28,12},{32,48},... | collective-permute-start | bytes 393224 | tf_op jit(solution)/shard_map/ppermute | solution.py:63
  114.6 2.7 %collective-permute-done.7 = bf16[4,128,128]{2,1,0:T(8,128)(2,1)S(1)} collective-permute-done((bf16[4,128,128]{2,1,0:T(8,128)(2,1)S(1)}, bf16[4,128,128]{2,1,0:T(8,128)(2,1)S(1)}, u32[]{:S(2)}, u32[]{:S(2)}) %collective-permute-start.7) | collective-permute-done | bytes 131104 | tf_op jit(solution)/shard_map/ppermute | solution.py:63
  117.5 1.8 collective-permute-start.9
  119.8 1.9 collective-permute-done.9
  121.8 3.1 %collective-permute-start.11 = (bf16[4,128,128]{2,1,0:T(8,128)(2,1)S(1)}, bf16[4,128,128]{2,1,0:T(8,128)(2,1)S(1)}, u32[]{:S(2)}, u32[]{:S(2)}) collective-permute-start(bf16[4,128,128]{2,1,0:T(8,128)(2,1)S(1)} %fusion.42), channel_id=1, source_target_pairs={{0,64},{4,68},{8,72},{12,76},{16,80},{20,84},{24,88},{28,92},{32,9... | collective-permute-start | bytes 393224 | tf_op jit(solution)/shard_map/ppermute | solution.py:63
  125.3 3.3 %collective-permute-done.11 = bf16[4,128,128]{2,1,0:T(8,128)(2,1)S(1)} collective-permute-done((bf16[4,128,128]{2,1,0:T(8,128)(2,1)S(1)}, bf16[4,128,128]{2,1,0:T(8,128)(2,1)S(1)}, u32[]{:S(2)}, u32[]{:S(2)}) %collective-permute-start.11) | collective-permute-done | bytes 131104 | tf_op jit(solution)/shard_map/ppermute | solution.py:63
  128.7 6.2 %collective-permute-start.13 = (bf16[4,128,128]{2,1,0:T(8,128)(2,1)S(1)}, bf16[4,128,128]{2,1,0:T(8,128)(2,1)S(1)}, u32[]{:S(2)}, u32[]{:S(2)}) collective-permute-start(bf16[4,128,128]{2,1,0:T(8,128)(2,1)S(1)} %fusion.39), channel_id=1, source_target_pairs={{0,128},{4,132},{8,136},{12,140},{16,144},{20,148},{24,152},{28,15... | collective-permute-start | bytes 393224 | tf_op jit(solution)/shard_map/ppermute | solution.py:63
  135.4 1.9 collective-permute-done.13
  137.8 1.1 multiply_reduce_fusion
  139.5 6.6 %convolution_convert_fusion = bf16[512,4096]{1,0:T(8,128)(2,1)} fusion(bf16[512,512]{0,1:T(8,128)(2,1)S(1)} %bitcast.203, bf16[512,4096]{1,0:T(8,128)(2,1)} %param.13), kind=kOutput, calls=%fused_computation.1 | convolution fusion | flops 2149580800 | bytes 8912896 | tf_op jit(solution)/shard_map/dot_general | solution.py:75
  146.1 53.0 %reduce-scatter.2.cloned.1.call-done = bf16[512,1024]{1,0:T(8,128)(2,1)} async-done(((bf16[512,4096]{1,0:T(8,128)(2,1)}), bf16[512,1024]{1,0:T(8,128)(2,1)}) %reduce-scatter.2.cloned.1.call-update) | async-done | bytes 1048592 | tf_op jit(solution)/shard_map/reduce_scatter | solution.py:131
  (85 shorter events, 13.9 us)
Async XLA Ops:
  6.5 74.5 %copy-start = (bf16[4096,128]{1,0:T(8,128)(2,1)S(1)}, bf16[4096,128]{1,0:T(8,128)(2,1)}, u32[]{:S(2)}) copy-start(bf16[4096,128]{1,0:T(8,128)(2,1)} %param.10) | copy-start | bytes 3145732
  6.5 192.6 %reduce-scatter.2.cloned.1.call-start = ((), (), s32[]{:S(2)}) async-start(), calls=%async_computation.1 | async-start | bytes 5242880 | tf_op jit(solution)/shard_map/reduce_scatter | solution.py:131
  6.5 24.6 %collective-permute-start = (bf16[512,1024]{1,0:T(8,128)(2,1)}, bf16[512,1024]{1,0:T(8,128)(2,1)S(1)}, u32[]{:S(2)}, u32[]{:S(2)}) collective-permute-start(bf16[512,1024]{1,0:T(8,128)(2,1)} %param.7), channel_id=1, source_target_pairs={{0,1},{1,2},{2,3},{3,0},{4,5},{5,6},{6,7},{7,4},{8,9},{9,10},{10,1... | collective-permute-start | bytes 3145736 | tf_op jit(solution)/shard_map/ppermute | solution.py:30
  8.7 40.5 %collective-permute-start.2 = (bf16[512,1024]{1,0:T(8,128)(2,1)}, bf16[512,1024]{1,0:T(8,128)(2,1)S(1)}, u32[]{:S(2)}, u32[]{:S(2)}) collective-permute-start(bf16[512,1024]{1,0:T(8,128)(2,1)} %param.7), channel_id=1, source_target_pairs={{1,0},{2,1},{3,2},{0,3},{5,4},{6,5},{7,6},{4,7},{9,8},{10,9},{11,1... | collective-permute-start | bytes 3145736 | tf_op jit(solution)/shard_map/ppermute | solution.py:33
  11.4 46.6 %copy-start.11 = (f32[4]{0:T(128)}, f32[4]{0:T(128)S(1)}, u32[]{:S(2)}) copy-start(f32[4]{0:T(128)S(1)} %slice_reduce_fusion) | copy-start | bytes 52
  11.5 21.3 %collective-permute-start.4 = (f32[4]{0:T(128)S(1)}, f32[4]{0:T(128)S(1)}, u32[]{:S(2)}, u32[]{:S(2)}) collective-permute-start(f32[4]{0:T(128)S(1)} %slice_reduce_fusion), channel_id=1, source_target_pairs={{0,4},{4,0},{8,12},{12,8},{16,20},{20,16},{24,28},{28,24},{32,36},... | collective-permute-start | bytes 56 | tf_op jit(solution)/shard_map/ppermute | solution.py:63
  16.8 0.6 copy-start.15
  31.2 23.6 %collective-permute-start.1 = (bf16[512,1024]{1,0:T(8,128)(2,1)S(1)}, bf16[512,1024]{1,0:T(8,128)(2,1)S(1)}, u32[]{:S(2)}, u32[]{:S(2)}) collective-permute-start(bf16[512,1024]{1,0:T(8,128)(2,1)S(1)} %collective-permute-done), channel_id=1, source_target_pairs={{0,1},{1,2},{2,3},{3,0},{4,5},{5,6},{6,7},{7,4},{8,9},{9,10},{10,1... | collective-permute-start | bytes 3145736 | tf_op jit(solution)/shard_map/ppermute | solution.py:30
  33.3 2.4 %collective-permute-start.6 = (f32[4]{0:T(128)S(1)}, f32[4]{0:T(128)S(1)}, u32[]{:S(2)}, u32[]{:S(2)}) collective-permute-start(f32[4]{0:T(128)S(1)} %get-tuple-element.50), channel_id=1, source_target_pairs={{0,8},{4,12},{8,0},{12,4},{16,24},{20,28},{24,16},{28,20},{32,40},... | collective-permute-start | bytes 56 | tf_op jit(solution)/shard_map/ppermute | solution.py:63
  36.2 3.9 %collective-permute-start.8 = (f32[4]{0:T(128)S(1)}, f32[4]{0:T(128)S(1)}, u32[]{:S(2)}, u32[]{:S(2)}) collective-permute-start(f32[4]{0:T(128)S(1)} %get-tuple-element.55), channel_id=1, source_target_pairs={{0,16},{4,20},{8,24},{12,28},{16,0},{20,4},{24,8},{28,12},{32,48},... | collective-permute-start | bytes 56 | tf_op jit(solution)/shard_map/ppermute | solution.py:63
  40.7 3.1 %collective-permute-start.10 = (f32[4]{0:T(128)S(1)}, f32[4]{0:T(128)S(1)}, u32[]{:S(2)}, u32[]{:S(2)}) collective-permute-start(f32[4]{0:T(128)S(1)} %get-tuple-element.45), channel_id=1, source_target_pairs={{0,32},{4,36},{8,40},{12,44},{16,48},{20,52},{24,56},{28,60},{32,0... | collective-permute-start | bytes 56 | tf_op jit(solution)/shard_map/ppermute | solution.py:63
  44.3 4.2 %collective-permute-start.12 = (f32[4]{0:T(128)S(1)}, f32[4]{0:T(128)S(1)}, u32[]{:S(2)}, u32[]{:S(2)}) collective-permute-start(f32[4]{0:T(128)S(1)} %get-tuple-element.43), channel_id=1, source_target_pairs={{0,64},{4,68},{8,72},{12,76},{16,80},{20,84},{24,88},{28,92},{32,9... | collective-permute-start | bytes 56 | tf_op jit(solution)/shard_map/ppermute | solution.py:63
  63.1 6.2 %copy-start.3 = (bf16[4096,36]{0,1:T(8,128)(2,1)S(1)}, bf16[4096,36]{0,1:T(8,128)(2,1)}, u32[]{:S(2)}) copy-start(bf16[4096,36]{0,1:T(8,128)(2,1)} %param.12) | copy-start | bytes 884740
  80.4 4.4 %copy-start.1 = (bf16[512,4,1024]{0,2,1:T(8,128)(2,1)S(1)}, bf16[512,4,1024]{0,2,1:T(8,128)(2,1)}, u32[]{:S(2)}) copy-start(bf16[512,4,1024]{0,2,1:T(8,128)(2,1)} %copy.101) | copy-start | bytes 12582916
  87.4 4.7 %copy-start.2 = (bf16[512,128]{1,0:T(8,128)(2,1)}, bf16[512,128]{1,0:T(8,128)(2,1)S(1)}, u32[]{:S(2)}) copy-start(bf16[512,128]{1,0:T(8,128)(2,1)S(1)} %convolution_convert_fusion.3) | copy-start | bytes 393220
  87.5 8.3 %slice-start = ((f32[4,2]{0,1:T(2,128)}), f32[4,1]{0,1:T(1,128)S(1)}, s32[]{:S(2)}) async-start(f32[4,2]{0,1:T(2,128)} %copy-done.15), calls=%async_computation.2 | async-start | bytes 1024 | tf_op jit(solution)/shard_map/slice | solution.py:115
  92.1 22.0 %copy-start.7 = (f32[4,512]{1,0:T(4,128)S(1)}, f32[4,512]{1,0:T(4,128)}, u32[]{:S(2)}) copy-start(f32[4,512]{1,0:T(4,128)} %get-tuple-element.33) | copy-start | bytes 24580
  92.1 11.2 %collective-permute-start.3 = (bf16[4,128,128]{2,1,0:T(8,128)(2,1)}, bf16[4,128,128]{2,1,0:T(8,128)(2,1)S(1)}, u32[]{:S(2)}, u32[]{:S(2)}) collective-permute-start(bf16[4,128,128]{2,1,0:T(8,128)(2,1)} %get-tuple-element.57), channel_id=1, source_target_pairs={{0,4},{4,0},{8,12},{12,8},{16,20},{20,16},{24,28},{28,24},{32,36},... | collective-permute-start | bytes 393224 | tf_op jit(solution)/shard_map/ppermute | solution.py:63
  95.9 21.4 %copy-start.9 = (f32[4]{0:T(128)S(1)}, f32[4]{0:T(128)}, u32[]{:S(2)}) copy-start(f32[4]{0:T(128)} %get-tuple-element.49) | copy-start | bytes 52
  95.9 21.4 %copy-start.10 = (f32[4]{0:T(128)S(1)}, f32[4]{0:T(128)}, u32[]{:S(2)}) copy-start(f32[4]{0:T(128)} %get-tuple-element.56) | copy-start | bytes 52
  95.9 21.4 %copy-start.13 = (f32[4]{0:T(128)S(1)}, f32[4]{0:T(128)}, u32[]{:S(2)}) copy-start(f32[4]{0:T(128)} %get-tuple-element.46) | copy-start | bytes 52
  98.5 20.8 %copy-start.6 = (f32[4,512]{1,0:T(4,128)S(1)}, f32[4,512]{1,0:T(4,128)}, u32[]{:S(2)}) copy-start(f32[4,512]{1,0:T(4,128)} %get-tuple-element.32) | copy-start | bytes 24580
  100.5 21.2 %copy-start.12 = (f32[4]{0:T(128)S(1)}, f32[4]{0:T(128)}, u32[]{:S(2)}) copy-start(f32[4]{0:T(128)} %get-tuple-element.44) | copy-start | bytes 52
  100.8 24.1 %copy-start.5 = (f32[4,512]{1,0:T(4,128)S(1)}, f32[4,512]{1,0:T(4,128)}, u32[]{:S(2)}) copy-start(f32[4,512]{1,0:T(4,128)} %get-tuple-element.31) | copy-start | bytes 24580
  103.3 25.3 %copy-start.14 = (f32[4]{0:T(128)S(1)}, f32[4]{0:T(128)}, u32[]{:S(2)}) copy-start(f32[4]{0:T(128)} %get-tuple-element.53) | copy-start | bytes 52
  104.0 30.9 %copy-start.4 = (f32[4,512]{1,0:T(4,128)S(1)}, f32[4,512]{1,0:T(4,128)}, u32[]{:S(2)}) copy-start(f32[4,512]{1,0:T(4,128)} %get-tuple-element.30) | copy-start | bytes 24580
  104.0 6.4 %collective-permute-start.5 = (bf16[4,128,128]{2,1,0:T(8,128)(2,1)S(1)}, bf16[4,128,128]{2,1,0:T(8,128)(2,1)S(1)}, u32[]{:S(2)}, u32[]{:S(2)}) collective-permute-start(bf16[4,128,128]{2,1,0:T(8,128)(2,1)S(1)} %fusion.76), channel_id=1, source_target_pairs={{0,8},{4,12},{8,0},{12,4},{16,24},{20,28},{24,16},{28,20},{32,40},... | collective-permute-start | bytes 393224 | tf_op jit(solution)/shard_map/ppermute | solution.py:63
  111.2 6.1 %collective-permute-start.7 = (bf16[4,128,128]{2,1,0:T(8,128)(2,1)S(1)}, bf16[4,128,128]{2,1,0:T(8,128)(2,1)S(1)}, u32[]{:S(2)}, u32[]{:S(2)}) collective-permute-start(bf16[4,128,128]{2,1,0:T(8,128)(2,1)S(1)} %fusion.43), channel_id=1, source_target_pairs={{0,16},{4,20},{8,24},{12,28},{16,0},{20,4},{24,8},{28,12},{32,48},... | collective-permute-start | bytes 393224 | tf_op jit(solution)/shard_map/ppermute | solution.py:63
  117.5 20.3 %copy-start.8 = (f32[4,512]{1,0:T(4,128)S(1)}, f32[4,512]{1,0:T(4,128)}, u32[]{:S(2)}) copy-start(f32[4,512]{1,0:T(4,128)} %get-tuple-element.28) | copy-start | bytes 24580
  117.5 4.1 %collective-permute-start.9 = (bf16[4,128,128]{2,1,0:T(8,128)(2,1)S(1)}, bf16[4,128,128]{2,1,0:T(8,128)(2,1)S(1)}, u32[]{:S(2)}, u32[]{:S(2)}) collective-permute-start(bf16[4,128,128]{2,1,0:T(8,128)(2,1)S(1)} %get-tuple-element.9), channel_id=1, source_target_pairs={{0,32},{4,36},{8,40},{12,44},{16,48},{20,52},{24,56},{28,60},{32,0... | collective-permute-start | bytes 393224 | tf_op jit(solution)/shard_map/ppermute | solution.py:63
  121.8 6.8 %collective-permute-start.11 = (bf16[4,128,128]{2,1,0:T(8,128)(2,1)S(1)}, bf16[4,128,128]{2,1,0:T(8,128)(2,1)S(1)}, u32[]{:S(2)}, u32[]{:S(2)}) collective-permute-start(bf16[4,128,128]{2,1,0:T(8,128)(2,1)S(1)} %fusion.42), channel_id=1, source_target_pairs={{0,64},{4,68},{8,72},{12,76},{16,80},{20,84},{24,88},{28,92},{32,9... | collective-permute-start | bytes 393224 | tf_op jit(solution)/shard_map/ppermute | solution.py:63
  128.7 8.6 %collective-permute-start.13 = (bf16[4,128,128]{2,1,0:T(8,128)(2,1)S(1)}, bf16[4,128,128]{2,1,0:T(8,128)(2,1)S(1)}, u32[]{:S(2)}, u32[]{:S(2)}) collective-permute-start(bf16[4,128,128]{2,1,0:T(8,128)(2,1)S(1)} %fusion.39), channel_id=1, source_target_pairs={{0,128},{4,132},{8,136},{12,140},{16,144},{20,148},{24,152},{28,15... | collective-permute-start | bytes 393224 | tf_op jit(solution)/shard_map/ppermute | solution.py:63
Sparse Core Ops, SparseCore 0:
  146.2 52.8 reduce-scatter.1
